TPU v7x, 512 devices: a whole 4x8x8 slice. The times are simulated.
512 devices in a mesh: dp: 16 (over y_lo, x, core), tensor: 32 (over y_hi, z).
Axes of the slice: x: 4, y: 8 (y_hi: 4, y_lo: 2; y = y_hi * 2 + y_lo), z: 8, core: 2. Of those that a mesh axis runs over, the one named last changes fastest.
Arguments:
- tokens: bfloat16 [1024, 6144], P('tensor', 'dp'), may hold values from -6 to 6
- in_weight: bfloat16 [6144, 24576], P('dp', 'tensor'), may hold values from -0.078125 to 0.078125
- out_weight: bfloat16 [24576, 6144], P('tensor', 'dp'), may hold values from -0.0390625 to 0.0390625
Outputs:
- teacher: bfloat16 [1024, 6144], P('tensor', 'dp')
- grad_in: float32 [6144, 24576], P('dp', 'tensor')
- grad_out: float32 [24576, 6144], P('tensor', 'dp')
All inputs are finite; a program needn't handle non-finite values.
Results may differ from a plain program's by a relative error of at most 0.038.
Values may be sent and summed in bfloat16 or wider, within the bound.
A program may use at most 64 MiB of HBM per device.

v0:
```python
import jax
import jax.numpy as jnp
from jax import lax
from jax.sharding import PartitionSpec as P

inv_root_two = 0.7071067811865476
inv_root_tau = 0.3989422804014327


def smooth_gate(values):
    return 0.5 * values * (1.0 + lax.erf(values * inv_root_two))


def gate_slope(values):
    return (
        0.5 * (1.0 + lax.erf(values * inv_root_two))
        + values * jnp.exp(-0.5 * values * values) * inv_root_tau
    )


def shards(tokens, in_weight, out_weight):
    tensor_size = lax.axis_size("tensor")
    everything = lax.all_gather(tokens, "tensor", axis=0, tiled=True)
    token_count = everything.shape[0]
    block_width = everything.shape[1]
    row_block = everything
    preact_local = lax.psum_scatter(
        jnp.dot(row_block, in_weight, preferred_element_type=jnp.float32).astype(jnp.bfloat16),
        "dp",
        scatter_dimension=0,
        tiled=True,
    )
    preact_all = lax.all_gather(preact_local, "dp", axis=0, tiled=True)
    pre_wide = preact_all.astype(jnp.float32)
    hidden = smooth_gate(pre_wide).astype(jnp.bfloat16)
    partial_value = jnp.dot(hidden, out_weight, preferred_element_type=jnp.float32)
    pieces = lax.all_to_all(
        partial_value[None].astype(jnp.bfloat16), "tensor", split_axis=1, concat_axis=0, tiled=True
    ).astype(jnp.float32)
    first_cut = tensor_size // 8
    second_cut = tensor_size // 4
    third_cut = tensor_size // 2
    student_one = jnp.sum(pieces[:first_cut], axis=0)
    student_two = student_one + jnp.sum(pieces[first_cut:second_cut], axis=0)
    student_three = student_two + jnp.sum(pieces[second_cut:third_cut], axis=0)
    full = student_three + jnp.sum(pieces[third_cut:], axis=0)
    factor = 1.0 / jnp.sqrt(jnp.float32(token_count))
    diff_one = (student_one - full) * factor
    diff_two = (student_two - full) * factor
    diff_three = (student_three - full) * factor
    cot_one = (diff_one + diff_two + diff_three).astype(jnp.bfloat16)
    cot_two = (diff_two + diff_three).astype(jnp.bfloat16)
    cot_three = diff_three.astype(jnp.bfloat16)
    piece_rows = pieces.shape[1]
    outbound = jnp.concatenate(
        [
            jnp.broadcast_to(cot_one[None], (first_cut, piece_rows, block_width)),
            jnp.broadcast_to(cot_two[None], (second_cut - first_cut, piece_rows, block_width)),
            jnp.broadcast_to(cot_three[None], (third_cut - second_cut, piece_rows, block_width)),
            jnp.zeros((tensor_size - third_cut, piece_rows, block_width), jnp.bfloat16),
        ],
        axis=0,
    )
    returned = lax.all_to_all(outbound, "tensor", split_axis=0, concat_axis=1, tiled=True)[0]
    grad_out = lax.dot_general(
        hidden, returned, (((0,), (0,)), ((), ())), preferred_element_type=jnp.float32
    )
    row_block = returned
    dhidden_local = lax.psum_scatter(
        lax.dot_general(
            row_block, out_weight, (((1,), (1,)), ((), ())), preferred_element_type=jnp.float32
        ).astype(jnp.bfloat16),
        "dp",
        scatter_dimension=0,
        tiled=True,
    ).astype(jnp.float32)
    dpre_local = (dhidden_local * gate_slope(preact_local.astype(jnp.float32))).astype(jnp.bfloat16)
    dpre_all = lax.all_gather(dpre_local, "dp", axis=0, tiled=True)
    grad_in = lax.dot_general(
        everything, dpre_all, (((0,), (0,)), ((), ())), preferred_element_type=jnp.float32
    )
    return (full.astype(jnp.bfloat16), grad_in, grad_out)


def solution(mesh):
    in_specs = (P("tensor", "dp"), P("dp", "tensor"), P("tensor", "dp"))
    out_specs = (P("tensor", "dp"), P("dp", "tensor"), P("tensor", "dp"))
    return jax.shard_map(shards, mesh=mesh, in_specs=in_specs, out_specs=out_specs, check_vma=False)
```

profile of v0, /device:TPU:1, one launch (start us, length us, event | category | flops | bytes accessed | tf_op | source)
XLA Modules:
  0.0 404.0 jit_solution(16604719426699818922)
XLA Ops:
  7.2 80.4 %all_gather.9 = bf16[1024,384]{1,0:T(8,128)(2,1)S(1)} all-gather(bf16[32,384]{1,0:T(8,128)(2,1)} %param.3), channel_id=1, replica_groups=mesh['dp'=16,'tensor'=32] {'tensor'}, dimensions={0}, use_global_device_ids=true | all-gather | bytes 811008 | tf_op jit(solution)/shard_map/all_gather | solution.py:23
  87.6 0.9 copy-done.3
  88.5 3.2 convolution_convert_fusion.1
  91.8 72.2 %reduce-scatter.3.cloned.1.call-done = bf16[64,768]{1,0:T(8,128)(2,1)} async-done(((bf16[1024,768]{1,0:T(8,128)(2,1)}), bf16[64,768]{1,0:T(8,128)(2,1)}) %reduce-scatter.3.cloned.1.call-update) | async-done | bytes 98320 | tf_op jit(solution)/shard_map/reduce_scatter | solution.py:27
  164.0 42.1 %all-gather.3.cloned.1.call-done = bf16[1024,768]{1,0:T(8,128)(2,1)} async-done(((bf16[64,768]{1,0:T(8,128)(2,1)}), bf16[1024,768]{1,0:T(8,128)(2,1)}) %all-gather.3.cloned.1.call-update) | async-done | bytes 1572880 | tf_op jit(solution)/shard_map/all_gather | solution.py:33
  206.0 1.8 fusion.1
  207.9 1.2 copy-done.1
  209.0 1.0 fusion.4
  210.0 1.2 copy.14
  211.8 5.4 %reduce = bf16[1024,384]{1,0:T(8,128)(2,1)S(1)} reduce(bf16[1024,1,384]{2,1,0:T(2,128)(2,1)S(1)} %bitcast.26, bf16[]{:T(256)} %broadcast.40), dimensions={1}, to_apply=%bitcast.22.reduce_sub_computation | reduce | bytes 1572866
  217.2 1.1 reshape.58
  218.3 12.0 %all-to-all-start = ((bf16[32,2,6144]{2,1,0:T(2,128)(2,1)}), bf16[32,2,6144]{2,1,0:T(2,128)(2,1)S(1)}, u32[]{:S(2)}, u32[]{:S(2)}) async-start(bf16[32,2,6144]{2,1,0:T(2,128)(2,1)} %reshape.58), calls=%async_computation.1 | async-start | bytes 1572864 | tf_op jit(solution)/shard_map/all_to_all | solution.py:37
  230.4 22.8 %all-to-all-done = bf16[32,2,6144]{2,1,0:T(2,128)(2,1)S(1)} async-done(((bf16[32,2,6144]{2,1,0:T(2,128)(2,1)}), bf16[32,2,6144]{2,1,0:T(2,128)(2,1)S(1)}, u32[]{:S(2)}, u32[]{:S(2)}) %all-to-all-start) | async-done | bytes 786464 | tf_op jit(solution)/shard_map/all_to_all | solution.py:37
  253.2 0.7 reshape.59
  254.7 0.8 slice.35
  256.7 28.7 %all_to_all.8 = bf16[32,32,384]{2,1,0:T(8,128)(2,1)S(1)} all-to-all(bf16[32,32,384]{2,1,0:T(8,128)(2,1)S(1)} %maximum_maximum_fusion), channel_id=1, replica_groups=mesh['dp'=16,'tensor'=32] {'tensor'}, dimensions={0} | all-to-all | bytes 1572864 | tf_op jit(solution)/shard_map/all_to_all | solution.py:64
  285.3 0.9 copy-done.5
  286.2 2.2 convolution_convert_fusion
  288.5 63.5 %reduce-scatter.5.cloned.1.call-done = bf16[64,768]{1,0:T(8,128)(2,1)} async-done(((bf16[1024,768]{1,0:T(8,128)(2,1)}), bf16[64,768]{1,0:T(8,128)(2,1)}) %reduce-scatter.5.cloned.1.call-update) | async-done | bytes 98320 | tf_op jit(solution)/shard_map/reduce_scatter | solution.py:69
  351.9 1.6 fusion.12
  353.6 3.2 fusion.15
  356.8 36.8 %all-gather.5.cloned.1.call-done = bf16[1024,768]{1,0:T(8,128)(2,1)} async-done(((bf16[64,768]{1,0:T(8,128)(2,1)}), bf16[1024,768]{1,0:T(8,128)(2,1)}) %all-gather.5.cloned.1.call-update) | async-done | bytes 1572880 | tf_op jit(solution)/shard_map/all_gather | solution.py:78
  393.7 2.4 convolution_bitcast_fusion
  396.1 1.4 copy.8
  (37 shorter events, 2.7 us)
Async XLA Ops:
  7.2 201.9 %copy-start = (bf16[768,384]{1,0:T(8,128)(2,1)S(1)}, bf16[768,384]{1,0:T(8,128)(2,1)}, u32[]{:S(2)}) copy-start(bf16[768,384]{1,0:T(8,128)(2,1)} %param.5) | copy-start | bytes 1769476
  7.2 156.8 %reduce-scatter.3.cloned.1.call-start = ((), (), s32[]{:S(2)}) async-start(), calls=%async_computation.4 | async-start | bytes 1671168 | tf_op jit(solution)/shard_map/reduce_scatter | solution.py:27
  87.6 0.9 copy-start.3
  91.7 114.3 %all-gather.3.cloned.1.call-start = ((), (), s32[]{:S(2)}) async-start(), calls=%async_computation.5 | async-start | bytes 1671168 | tf_op jit(solution)/shard_map/all_gather | solution.py:33
  207.9 1.2 copy-start.1
  218.3 34.9 %all-to-all-start = ((bf16[32,2,6144]{2,1,0:T(2,128)(2,1)}), bf16[32,2,6144]{2,1,0:T(2,128)(2,1)S(1)}, u32[]{:S(2)}, u32[]{:S(2)}) async-start(bf16[32,2,6144]{2,1,0:T(2,128)(2,1)} %reshape.58), calls=%async_computation.1 | async-start | bytes 1572864 | tf_op jit(solution)/shard_map/all_to_all | solution.py:37
  230.2 121.7 %reduce-scatter.5.cloned.1.call-start = ((), (), s32[]{:S(2)}) async-start(), calls=%async_computation.6 | async-start | bytes 1671168 | tf_op jit(solution)/shard_map/reduce_scatter | solution.py:69
  285.3 0.9 copy-start.5
  286.2 65.7 %copy-start.6 = (bf16[64,768]{1,0:T(8,128)(2,1)S(1)}, bf16[64,768]{1,0:T(8,128)(2,1)}, u32[]{:S(2)}) copy-start(bf16[64,768]{1,0:T(8,128)(2,1)} %reduce-scatter.3.cloned.1.call-done) | copy-start | bytes 294916
  288.4 65.2 %copy-start.2 = (bf16[1024,768]{1,0:T(8,128)(2,1)S(1)}, bf16[1024,768]{1,0:T(8,128)(2,1)}, u32[]{:S(2)}) copy-start(bf16[1024,768]{1,0:T(8,128)(2,1)} %copy-done.1) | copy-start | bytes 4718596
  288.4 105.2 %all-gather.5.cloned.1.call-start = ((), (), s32[]{:S(2)}) async-start(), calls=%async_computation.7 | async-start | bytes 1671168 | tf_op jit(solution)/shard_map/all_gather | solution.py:78
  353.6 40.1 %copy-start.4 = (bf16[1024,384]{1,0:T(8,128)(2,1)S(1)}, bf16[1024,384]{1,0:T(8,128)(2,1)}, u32[]{:S(2)}) copy-start(bf16[1024,384]{1,0:T(8,128)(2,1)} %copy-done.3) | copy-start | bytes 2359300
Sparse Core Ops, SparseCore 0:
  91.9 72.0 reduce-scatter.2
  166.3 39.6 all-gather.2
  288.5 63.3 reduce-scatter.4
  353.9 39.6 all-gather.4
where the time goes:
time: 404 us
  waiting for transfers between devices  237 us (59%)
  blocking collectives  109 us (27%)
  between operations  14 us (3%)
  starting transfers between devices  12.1 us (3%)
  matrix products  12 us (3%)
  other arithmetic  9.77 us (2%)
  local copies, waits for them, and re-layouts  9.71 us (2%)
    all_gather x1, blocking collectives, shards(): everything = lax.all_gather(tokens, 'tensor', axis=0, tiled=True)  80.4 us
    reduce_scatter x1, waiting for transfers between devices, shards(): lax.psum_scatter(jnp.dot(row_block, in_weight, preferred_element_type=jnp...  72.2 us
    reduce_scatter x1, waiting for transfers between devices, shards(): lax.psum_scatter(lax.dot_general(row_block, out_weight, (((1,), (1,)), ((...  63.5 us
    all_gather x1, waiting for transfers between devices, shards(): preact_all = lax.all_gather(preact_local, 'dp', axis=0, tiled=True)  42.1 us
    all_gather x1, waiting for transfers between devices, shards(): dpre_all = lax.all_gather(dpre_local, 'dp', axis=0, tiled=True)  36.8 us
    all_to_all x1, blocking collectives, shards(): lax.all_to_all(outbound, 'tensor', split_axis=0, concat_axis=1, tiled=True)  28.7 us
    all_to_all x1, waiting for transfers between devices, shards(): lax.all_to_all(partial_value[None].astype(jnp.bfloat16), 'tensor', split_...  22.8 us
    all_to_all x1, starting transfers between devices, shards(): lax.all_to_all(partial_value[None].astype(jnp.bfloat16), 'tensor', split_...  12 us
  transfers between devices with their start and end apart: 5, of which 5 were waited for; matrix products, arithmetic and copies ran while one was open for 1% of the time, Pallas kernels for 0%

commit v1 on v0

v1 whole, which is shorter than its diff:
```python
import functools

import jax
import jax.numpy as jnp
from jax import lax
from jax.experimental import pallas as pl
from jax.experimental.pallas import tpu as pltpu
from jax.sharding import PartitionSpec as P

inv_root_two = 0.7071067811865476
inv_root_tau = 0.3989422804014327
MESH = pl.DeviceIdType.MESH
BF16 = jnp.bfloat16
F32 = jnp.float32


def smooth_gate(values):
    return 0.5 * values * (1.0 + lax.erf(values * inv_root_two))


def gate_slope(values):
    return (
        0.5 * (1.0 + lax.erf(values * inv_root_two))
        + values * jnp.exp(-0.5 * values * values) * inv_root_tau
    )


def rows(start, size):
    return pl.ds(pl.multiple_of(start, size), size)


def kernel(
    tok_ref, win_hbm, wout_hbm,
    teacher_ref, gin_ref, gout_ref,
    win, wout, tok_all, slope,
    keep, give, sib_in, summed, rs_in,
    hid, contrib, pieces, cots, cot_all,
    keep2, give2, sib_in2, summed2, rs_in2, dpre,
    wsem, ta_s, ta_r, a2_s, a2_r, ct_s, ct_r,
    sb_s, sb_r, rs_s, rs_r, ag_s, ag_r, rl_s, rl_r,
    sb2_s, sb2_r, rs2_s, rs2_r, ag2_s, ag2_r, rl2_s, rl2_r,
):
    d = lax.axis_index("dp")
    t = lax.axis_index("tensor")
    chip = d // 2
    core = d % 2
    other = 1 - core
    sib = chip * 2 + other
    y_hi = t // 8
    z = t % 8

    def remote(src, dst, s_sem, r_sem, dev):
        return pltpu.make_async_remote_copy(
            src_ref=src, dst_ref=dst, send_sem=s_sem, recv_sem=r_sem,
            device_id=dev, device_id_type=MESH,
        )

    w1 = pltpu.make_async_copy(win_hbm, win, wsem.at[0])
    w2 = pltpu.make_async_copy(wout_hbm, wout, wsem.at[1])
    w1.start()
    w2.start()

    barrier = pltpu.get_barrier_semaphore()

    @pl.loop(1, 32)
    def _(i):
        pl.semaphore_signal(barrier, inc=1, device_id={"tensor": (t + i) % 32}, device_id_type=MESH)

    @pl.loop(1, 8)
    def _(i):
        pl.semaphore_signal(
            barrier, inc=1, device_id={"dp": ((chip + i) % 8) * 2 + core}, device_id_type=MESH
        )

    pl.semaphore_signal(barrier, inc=1, device_id={"dp": sib}, device_id_type=MESH)
    tok_all[rows(t * 32, 32), :] = tok_ref[...]
    pl.semaphore_wait(barrier, 39)

    def tok_copy(dst, src_t):
        return remote(
            tok_ref, tok_all.at[rows(src_t * 32, 32)], ta_s.at[dst], ta_r.at[src_t], {"tensor": dst}
        )

    @pl.loop(1, 32)
    def _(i):
        dst = ((y_hi + i % 4) % 4) * 8 + (z + i // 4) % 8
        tok_copy(dst, t).start()

    w1.wait()
    w2.wait()

    def reduce_scatter(ready, block, keep, give, sib_in, summed, rs_in, sb_s, sb_r, rs_s, rs_r):
        def sib_copy(g):
            return remote(give.at[g], sib_in.at[g], sb_s.at[g], sb_r.at[g], {"dp": sib})

        def out_copy(g, src):
            return remote(
                summed.at[g], rs_in.at[src], rs_s.at[g], rs_r.at[src], {"dp": g * 2 + core}
            )

        @pl.loop(0, 9)
        def _(i):
            @pl.when(i < 8)
            def _():
                g = (chip + 1 + i) % 8
                ready(g)
                term = block(g).astype(BF16)
                first, second = term[:64], term[64:]
                mine = core == 0
                keep[g] = jnp.where(mine, first, second)
                give[g] = jnp.where(mine, second, first)
                sib_copy(g).start()

            @pl.when(i > 0)
            def _():
                g = (chip + i) % 8
                sib_copy(g).wait_recv()
                total = (keep[g].astype(F32) + sib_in[g].astype(F32)).astype(BF16)
                summed[g] = total

                @pl.when(g != chip)
                def _():
                    out_copy(g, chip).start()

                @pl.when(g == chip)
                def _():
                    rs_in[g] = total

        @pl.loop(0, 8)
        def _(g):
            sib_copy(g).wait_send()

        @pl.loop(1, 8)
        def _(i):
            out_copy((chip + i) % 8, (chip + 8 - i) % 8).wait()

        total = jnp.zeros((64, 768), F32)
        for g in range(8):
            total = total + rs_in[g].astype(F32)
        return total

    def gather(buf, use, ag_s, ag_r, rl_s, rl_r):
        def out_copy(g, src):
            place = buf.at[rows((src * 2 + core) * 64, 64)]
            return remote(place, place, ag_s.at[g], ag_r.at[src], {"dp": g * 2 + core})

        def relay(src, which):
            place = buf.at[rows((src * 2 + which) * 64, 64)]
            return remote(place, place, rl_s.at[src], rl_r.at[src], {"dp": sib})

        @pl.loop(1, 8)
        def _(i):
            out_copy((chip + i) % 8, chip).start()

        @pl.loop(0, 9)
        def _(i):
            @pl.when(i < 8)
            def _():
                src = (chip + 8 - i) % 8

                @pl.when(i > 0)
                def _():
                    out_copy(chip, src).wait_recv()

                relay(src, core).start()

            @pl.when(i > 0)
            def _():
                src = (chip + 9 - i) % 8
                relay(src, other).wait_recv()
                use(src)

        @pl.loop(0, 8)
        def _(g):
            relay(g, core).wait_send()

        @pl.loop(1, 8)
        def _(i):
            out_copy((chip + i) % 8, chip).wait_send()

    def tok_ready(g):
        @pl.loop(0, 4)
        def _(j):
            src = g * 4 + j

            @pl.when(src != t)
            def _():
                tok_copy(t, src).wait_recv()

    def up(g):
        return jnp.dot(tok_all[rows(g * 128, 128), :], win[...], preferred_element_type=F32)

    pre = reduce_scatter(
        tok_ready, up, keep, give, sib_in, summed, rs_in, sb_s, sb_r, rs_s, rs_r
    )
    pre = pre.astype(BF16).astype(F32)
    slope[...] = gate_slope(pre)
    hid[rows(d * 64, 64), :] = smooth_gate(pre).astype(BF16)

    @pl.loop(1, 32)
    def _(i):
        tok_copy((t + i) % 32, t).wait_send()

    def piece_copy(dst, src_t):
        return remote(
            contrib.at[rows(dst * 32, 32)], pieces.at[src_t], a2_s.at[dst], a2_r.at[src_t],
            {"tensor": dst},
        )

    def down(g):
        contrib[rows(g * 128, 128), :] = jnp.dot(
            hid[rows(g * 128, 128), :], wout[...], preferred_element_type=F32
        ).astype(BF16)

        @pl.loop(0, 4)
        def _(j):
            dst = g * 4 + j

            @pl.when(dst != t)
            def _():
                piece_copy(dst, t).start()

            @pl.when(dst == t)
            def _():
                pieces[t] = contrib[rows(t * 32, 32), :]

    gather(hid, down, ag_s, ag_r, rl_s, rl_r)

    @pl.loop(1, 32)
    def _(i):
        piece_copy((t + i) % 32, (t + 32 - i) % 32).wait()

    def segment(low, high):
        return lax.fori_loop(
            low, high, lambda s, acc: acc + pieces[s].astype(F32), jnp.zeros((32, 384), F32)
        )

    student_one = segment(0, 4)
    student_two = student_one + segment(4, 8)
    student_three = student_two + segment(8, 16)
    full = student_three + segment(16, 32)
    factor = 1.0 / 32.0
    diff_one = (student_one - full) * factor
    diff_two = (student_two - full) * factor
    diff_three = (student_three - full) * factor
    cots[0] = (diff_one + diff_two + diff_three).astype(BF16)
    cots[1] = (diff_two + diff_three).astype(BF16)
    cots[2] = diff_three.astype(BF16)

    def range_of(unit_block):
        return unit_block // 4 - unit_block // 12

    def cot_copy(dst, src_t):
        return remote(
            cots.at[range_of(dst)], cot_all.at[rows(src_t * 32, 32)], ct_s.at[dst], ct_r.at[src_t],
            {"tensor": dst},
        )

    @pl.loop(0, 16)
    def _(i):
        dst = (t + 1 + i) % 16

        @pl.when(dst != t)
        def _():
            cot_copy(dst, t).start()

    teacher_ref[...] = full.astype(BF16)

    @pl.when(t < 16)
    def _():
        cot_all[rows(t * 32, 32), :] = cots[range_of(t)]

        def cot_ready(g):
            @pl.loop(0, 4)
            def _(j):
                src = g * 4 + j

                @pl.when(src != t)
                def _():
                    cot_copy(t, src).wait_recv()

        def back(g):
            return lax.dot_general(
                cot_all[rows(g * 128, 128), :], wout[...], (((1,), (1,)), ((), ())),
                preferred_element_type=F32,
            )

        dhidden = reduce_scatter(
            cot_ready, back, keep2, give2, sib_in2, summed2, rs_in2, sb2_s, sb2_r, rs2_s, rs2_r
        )
        dpre[rows(d * 64, 64), :] = (dhidden * slope[...]).astype(BF16)
        gather(dpre, lambda g: None, ag2_s, ag2_r, rl2_s, rl2_r)
        gin_ref[...] = lax.dot_general(
            tok_all[...], dpre[...], (((0,), (0,)), ((), ())), preferred_element_type=F32
        )
        gout_ref[...] = lax.dot_general(
            hid[...], cot_all[...], (((0,), (0,)), ((), ())), preferred_element_type=F32
        )

    @pl.when(t >= 16)
    def _():
        gin_ref[...] = jnp.zeros_like(gin_ref)
        gout_ref[...] = jnp.zeros_like(gout_ref)

    @pl.loop(0, 16)
    def _(i):
        @pl.when(i != t)
        def _():
            cot_copy(i, t).wait_send()


def shards(tokens, in_weight, out_weight):
    vmem = pl.BlockSpec(memory_space=pltpu.VMEM)
    hbm = pl.BlockSpec(memory_space=pl.ANY)
    dma = pltpu.SemaphoreType.DMA
    block = pltpu.VMEM((8, 64, 768), BF16)
    return pl.pallas_call(
        kernel,
        out_shape=(
            jax.ShapeDtypeStruct((32, 384), BF16),
            jax.ShapeDtypeStruct((384, 768), F32),
            jax.ShapeDtypeStruct((768, 384), F32),
        ),
        in_specs=[vmem, hbm, hbm],
        out_specs=(vmem, vmem, vmem),
        scratch_shapes=[
            pltpu.VMEM((384, 768), BF16),
            pltpu.VMEM((768, 384), BF16),
            pltpu.VMEM((1024, 384), BF16),
            pltpu.VMEM((64, 768), F32),
            block, block, block, block, block,
            pltpu.VMEM((1024, 768), BF16),
            pltpu.VMEM((1024, 384), BF16),
            pltpu.VMEM((32, 32, 384), BF16),
            pltpu.VMEM((3, 32, 384), BF16),
            pltpu.VMEM((1024, 384), BF16),
            block, block, block, block, block,
            pltpu.VMEM((1024, 768), BF16),
            dma((2,)),
        ]
        + [dma((32,))] * 6
        + [dma((8,))] * 16,
        compiler_params=pltpu.CompilerParams(
            collective_id=0, has_side_effects=True, vmem_limit_bytes=48 * 1024 * 1024
        ),
        cost_estimate=pl.CostEstimate(
            flops=5 * 2 * 1024 * 384 * 768, bytes_accessed=4_000_000, transcendentals=100_000
        ),
    )(tokens, in_weight, out_weight)


def solution(mesh):
    in_specs = (P("tensor", "dp"), P("dp", "tensor"), P("tensor", "dp"))
    out_specs = (P("tensor", "dp"), P("dp", "tensor"), P("tensor", "dp"))
    return jax.shard_map(shards, mesh=mesh, in_specs=in_specs, out_specs=out_specs, check_vma=False)
```

time: 404 us -> 149 us (0.37)
  waiting for transfers between devices: 237 us -> 0 us
  Pallas kernels: 0 us -> 142 us
  blocking collectives: 109 us -> 0 us
  between operations: 14 us -> 0.65 us
  starting transfers between devices: 12.1 us -> 0 us
  matrix products: 12 us -> 0 us
  other arithmetic: 9.77 us -> 0 us
  local copies, waits for them, and re-layouts: 9.71 us -> 5.49 us
    pallas_call x0 -> x1, Pallas kernels: none -> 142 us  [shards(): pl.pallas_call(kernel, out_shape=(jax.ShapeDtypeStruct((32, 384), BF16),...]
    reduce_scatter x2 -> x0, waiting for transfers between devices: 136 us -> none  [the longest x1 72.2 us: shards(): lax.psum_scatter(jnp.dot(row_block, in_weight, preferred_element_type=jnp...]
    all_gather x1 -> x0, blocking collectives: 80.4 us -> none  [shards(): everything = lax.all_gather(tokens, 'tensor', axis=0, tiled=True)]
    all_gather x2 -> x0, waiting for transfers between devices: 78.9 us -> none  [the longest x1 42.1 us: shards(): preact_all = lax.all_gather(preact_local, 'dp', axis=0, tiled=True)]
    all_to_all x1 -> x0, blocking collectives: 28.7 us -> none  [shards(): lax.all_to_all(outbound, 'tensor', split_axis=0, concat_axis=1, tiled=True)]
    all_to_all x1 -> x0, waiting for transfers between devices: 22.8 us -> none  [shards(): lax.all_to_all(partial_value[None].astype(jnp.bfloat16), 'tensor', split_...]
    dot_general x5 -> x0, matrix products: 12 us -> none  [the longest x1 3.22 us: shards(): lax.dot_general(hidden, returned, (((0,), (0,)), ((), ())), preferred_ele...]
    all_to_all x1 -> x0, starting transfers between devices: 12 us -> none  [shards(): lax.all_to_all(partial_value[None].astype(jnp.bfloat16), 'tensor', split_...]
  transfers between devices with their start and end apart: 5 -> 0, of which waited for: 5 -> 0; matrix products, arithmetic and copies ran while one was open for 1% -> 0% of each run, Pallas kernels for 0% -> 0%
where the time goes in v1:
time: 149 us; the launch traced here: 148 us
  Pallas kernels  142 us (95%)
  local copies, waits for them, and re-layouts  5.49 us (4%)
    pallas_call x1, Pallas kernels, shards(): pl.pallas_call(kernel, out_shape=(jax.ShapeDtypeStruct((32, 384), BF16),...  142 us
    unnamed x9, local copies, waits for them, and re-layouts  5.49 us

profile of v1, /device:TPU:1, one launch (start us, length us, event | category | flops | bytes accessed | tf_op | source)
XLA Modules:
  0.0 147.9 jit_solution(7481431751838112117)
XLA Ops:
  0.6 0.0 copy-start
  0.6 1.1 copy-done
  1.7 0.0 copy-start.1
  1.7 1.1 copy-done.1
  2.8 0.0 copy-start.2
  2.8 0.7 copy-done.2
  3.5 141.8 %shard_map.58 = (bf16[32,384]{1,0:T(8,128)(2,1)S(1)}, f32[384,768]{1,0:T(8,128)S(1)}, f32[768,384]{1,0:T(8,128)S(1)}) custom-call(bf16[32,384]{1,0:T(8,128)(2,1)S(1)} %copy-done.2, bf16[384,768]{1,0:T(8,128)(2,1)S(1)} %copy-done, bf16[768,384]{1,0:T(8,128)(2,1)S(1)} %copy-done.1), custom_call_target="tpu_custom_call" | custom-call | flops 3019898880 | bytes 4000000 | tf_op jit(solution)/shard_map/pallas_call | solution.py:317
  145.3 0.6 copy.9
  145.9 1.0 copy.10
  146.9 1.0 copy.11
Async XLA Ops:
  0.6 1.1 copy-start
  1.7 1.1 copy-start.1
  2.8 0.7 copy-start.2

commit v2 on v0

v2 whole, which is shorter than its diff:
```python
import jax
import jax.numpy as jnp
from jax import lax
from jax.experimental import pallas as pl
from jax.experimental.pallas import tpu as pltpu
from jax.sharding import PartitionSpec as P

inv_root_two = 0.7071067811865476
inv_root_tau = 0.3989422804014327
MESH = pl.DeviceIdType.MESH
BF16 = jnp.bfloat16
F32 = jnp.float32
LAG_SUM, LAG_HID, LAG_ALL, LAG_USE = 1, 4, 7, 8


def smooth_gate(values):
    return 0.5 * values * (1.0 + lax.erf(values * inv_root_two))


def gate_slope(values):
    return (
        0.5 * (1.0 + lax.erf(values * inv_root_two))
        + values * jnp.exp(-0.5 * values * values) * inv_root_tau
    )


def rows(start, size, step=None):
    return pl.ds(pl.multiple_of(start, step or size), size)


def kernel(
    tok_hbm, win_hbm, wout_hbm,
    teacher_ref, gin_ref, gout_ref,
    win, wout, tok_all, slope, hid, contrib, z_in, y_out, y_in,
    cots, cot_y, cot_all, dpre,
    keep, give, sib_in, summed, rs_in,
    keep2, give2, sib_in2, summed2, rs_in2,
    wsem, tok_s, tok_r, zin_s, zin_r, yin_s, yin_r, cy_s, cy_r, ct_s, ct_r,
    sb_s, sb_r, rs_s, rs_r, ag_s, ag_r, rl_s, rl_r,
    sb2_s, sb2_r, rs2_s, rs2_r, ag2_s, ag2_r, rl2_s, rl2_r,
):
    d = lax.axis_index("dp")
    t = lax.axis_index("tensor")
    chip = d // 2
    core = d % 2
    sib = chip * 2 + 1 - core
    y = t // 8
    z = t % 8

    def remote(src, dst, s_sem, r_sem, dev):
        return pltpu.make_async_remote_copy(
            src_ref=src, dst_ref=dst, send_sem=s_sem, recv_sem=r_sem,
            device_id=dev, device_id_type=MESH,
        )

    def drain_send(ref, sem):
        remote(ref, ref, sem, sem, {"dp": sib}).wait_send()

    def drain_recv(ref, sem):
        remote(ref, ref, sem, sem, {"dp": sib}).wait_recv()

    def offset(i):
        n = (8 - i) % 8
        return ((n + 1) // 2) * (2 * (n % 2) - 1)

    def along_z(i):
        return (z + offset(i) + 8) % 8

    mine = tok_all.at[rows(y * 32, 32)]
    w0 = pltpu.make_async_copy(tok_hbm, mine, wsem.at[0])
    w1 = pltpu.make_async_copy(win_hbm, win, wsem.at[1])
    w2 = pltpu.make_async_copy(wout_hbm, wout, wsem.at[2])
    w0.start()
    w1.start()
    w2.start()

    barrier = pltpu.get_barrier_semaphore()

    @pl.loop(1, 8)
    def _(i):
        pl.semaphore_signal(
            barrier, inc=1, device_id={"tensor": y * 8 + (z + i) % 8}, device_id_type=MESH
        )
        pl.semaphore_signal(
            barrier, inc=1, device_id={"dp": ((chip + i) % 8) * 2 + core}, device_id_type=MESH
        )

    @pl.loop(1, 4)
    def _(i):
        pl.semaphore_signal(
            barrier, inc=1, device_id={"tensor": ((y + i) % 4) * 8 + z}, device_id_type=MESH
        )

    pl.semaphore_signal(barrier, inc=1, device_id={"dp": sib}, device_id_type=MESH)
    w0.wait()
    pl.semaphore_wait(barrier, 18)

    def chunk_to(i, k, src, all_ref, s_sem, r_sem):
        return remote(
            src, all_ref.at[rows(i * 128 + k * 32, 32)], s_sem, r_sem.at[i],
            {"tensor": y * 8 + along_z(i)},
        )

    @pl.loop(1, 4)
    def _(j):
        k = (y + 1 + j % 3) % 4
        remote(mine, mine, tok_s, tok_r.at[0], {"tensor": k * 8 + z}).start()

    @pl.loop(1, 8)
    def _(i):
        chunk_to(i, y, mine, tok_all, tok_s, tok_r).start()

    drain_recv(tok_all.at[rows(0, 96)], tok_r.at[0])

    @pl.loop(1, 8)
    def _(i):
        @pl.loop(1, 4)
        def _(j):
            k = (y + j) % 4
            chunk_to(i, k, tok_all.at[rows(k * 32, 32)], tok_all, tok_s, tok_r).start()

    w1.wait()
    w2.wait()

    def pipeline(
        ready, block, finish, use, full_buf,
        keep, give, sib_in, summed, rs_in, sb_s, sb_r, rs_s, rs_r, ag_s, ag_r, rl_s, rl_r,
    ):
        def sib_copy(i):
            return remote(give.at[i], sib_in.at[i], sb_s, sb_r.at[i], {"dp": sib})

        def relay(i):
            place = full_buf.at[core, rows(i * 128, 128)]
            return remote(place, place, rl_s, rl_r.at[i], {"dp": sib})

        @pl.loop(0, 8 + LAG_USE)
        def _(s):
            @pl.when(s < 8)
            def _():
                ready(s)
                term = block(s).astype(BF16)
                first, second = term[:, :384], term[:, 384:]
                keep[s] = jnp.where(core == 0, first, second)
                give[s] = jnp.where(core == 0, second, first)
                sib_copy(s).start()

            @pl.when((s >= LAG_SUM) & (s < LAG_SUM + 8))
            def _():
                i = s - LAG_SUM
                sib_copy(i).wait_recv()
                total = (keep[i].astype(F32) + sib_in[i].astype(F32)).astype(BF16)
                summed[rows(i * 128, 128), :] = total

                @pl.loop(1, 8)
                def _(j):
                    c = (chip + j) % 8
                    remote(
                        summed.at[rows(i * 128 + c * 16, 16)],
                        rs_in.at[rows(i * 128 + chip * 16, 16)],
                        rs_s, rs_r.at[i], {"dp": c * 2 + core},
                    ).start()

                own = rows(i * 128 + chip * 16, 16)
                rs_in[own, :] = summed[own, :]

            @pl.when((s >= LAG_HID) & (s < LAG_HID + 8))
            def _():
                i = s - LAG_HID
                drain_recv(rs_in.at[rows(i * 128, 112, 128)], rs_r.at[i])
                total = jnp.zeros((16, 384), F32)
                for c in range(8):
                    total = total + rs_in[rows(i * 128 + c * 16, 16), :].astype(F32)
                own = rows(i * 128 + chip * 16, 16)
                full_buf[core, own, :] = finish(i, total)
                place = full_buf.at[core, own]

                @pl.loop(1, 8)
                def _(j):
                    c = (chip + j) % 8
                    remote(place, place, ag_s, ag_r.at[i], {"dp": c * 2 + core}).start()

            @pl.when((s >= LAG_ALL) & (s < LAG_ALL + 8))
            def _():
                i = s - LAG_ALL
                drain_recv(full_buf.at[core, rows(i * 128, 112, 128)], ag_r.at[i])
                relay(i).start()

            @pl.when(s >= LAG_USE)
            def _():
                i = s - LAG_USE
                relay(i).wait_recv()
                use(i)

        drain_send(give, sb_s)
        drain_send(summed.at[rows(0, 896)], rs_s)
        drain_send(full_buf.at[0, rows(0, 896)], ag_s)
        drain_send(full_buf.at[0], rl_s)

    def tok_ready(i):
        @pl.when(i > 0)
        def _():
            drain_recv(tok_all.at[rows(i * 128, 128)], tok_r.at[i])

    def up(i):
        return jnp.dot(tok_all[rows(i * 128, 128), :], win[...], preferred_element_type=F32)

    def hidden_of(i, total):
        pre = total.astype(BF16).astype(F32)
        slope[i] = gate_slope(pre)
        return smooth_gate(pre).astype(BF16)

    def down(i):
        group = rows(i * 128, 128)
        out = jnp.dot(hid[0, group, :], wout[:384, :], preferred_element_type=F32)
        out = out + jnp.dot(hid[1, group, :], wout[384:, :], preferred_element_type=F32)

        @pl.when(i == 0)
        def _():
            z_in[z] = out.astype(BF16)

        @pl.when(i > 0)
        def _():
            contrib[i] = out.astype(BF16)
            dst = (z - offset(i) + 8) % 8
            remote(contrib.at[i], z_in.at[z], zin_s, zin_r, {"tensor": y * 8 + dst}).start()

    pipeline(
        tok_ready, up, hidden_of, down, hid,
        keep, give, sib_in, summed, rs_in, sb_s, sb_r, rs_s, rs_r, ag_s, ag_r, rl_s, rl_r,
    )

    drain_recv(z_in.at[pl.ds(0, 7)], zin_r)

    def y_copy(which, k, slot):
        return remote(
            y_out.at[which, k], y_in.at[slot], yin_s.at[which, k], yin_r.at[slot],
            {"tensor": k * 8 + z},
        )

    slot = y + (y + 3) // 4

    @pl.loop(0, 4)
    def _(j):
        k = (y + 2 + j + j // 2 + j // 3 * 2) % 4
        part = rows(k * 32, 32)
        low = jnp.zeros((32, 384), F32)
        high = jnp.zeros((32, 384), F32)
        for s in range(4):
            low = low + z_in[s, part, :].astype(F32)
            high = high + z_in[s + 4, part, :].astype(F32)

        @pl.when(y == 0)
        def _():
            y_out[0, k] = low.astype(BF16)
            y_out[1, k] = high.astype(BF16)

        @pl.when(y > 0)
        def _():
            y_out[0, k] = (low + high).astype(BF16)

        @pl.when(k != y)
        def _():
            y_copy(0, k, slot).start()

            @pl.when(y == 0)
            def _():
                y_copy(1, k, 1).start()

        @pl.when(k == y)
        def _():
            y_in[slot] = y_out[0, k]

            @pl.when(y == 0)
            def _():
                y_in[1] = y_out[1, k]

    @pl.loop(0, 5)
    def _(s):
        @pl.when(s - (s + 4) // 5 != y)
        def _():
            y_copy(0, y, s).wait_recv()

    student_one = y_in[0].astype(F32)
    student_two = student_one + y_in[1].astype(F32)
    student_three = student_two + y_in[2].astype(F32)
    full = student_three + (y_in[3].astype(F32) + y_in[4].astype(F32))
    factor = 1.0 / 32.0
    diff_one = (student_one - full) * factor
    diff_two = (student_two - full) * factor
    diff_three = (student_three - full) * factor
    cots[0] = (diff_one + diff_two + diff_three).astype(BF16)
    cots[1] = (diff_two + diff_three).astype(BF16)
    cots[2] = diff_three.astype(BF16)

    def cot_y_copy(which):
        dst = which // 2
        return remote(
            cots.at[which], cot_y.at[which % 2, rows(y * 32, 32)], cy_s.at[which],
            cy_r.at[which % 2, y], {"tensor": dst * 8 + z},
        )

    for which in range(3):
        @pl.when(y != which // 2)
        def _(which=which):
            cot_y_copy(which).start()

        @pl.when(y == which // 2)
        def _(which=which):
            cot_y[which % 2, rows(y * 32, 32), :] = cots[which]

    teacher_ref[...] = full.astype(BF16)

    @pl.when(y < 2)
    def _():
        def cot_chunk(i, k):
            kind = (1 - y) * (along_z(i) // 4)
            return chunk_to(i, k, cot_y.at[kind, rows(k * 32, 32)], cot_all, ct_s, ct_r)

        @pl.loop(1, 8)
        def _(i):
            cot_chunk(i, y).start()

        @pl.loop(1, 4)
        def _(j):
            k = (y + j) % 4
            part = cot_y.at[0, rows(k * 32, 32)]
            drain_recv(part, cy_r.at[0, k])

            @pl.when(y == 0)
            def _():
                drain_recv(part, cy_r.at[1, k])

        @pl.loop(1, 8)
        def _(i):
            @pl.loop(1, 4)
            def _(j):
                cot_chunk(i, (y + j) % 4).start()

        cot_all[rows(0, 128), :] = cot_y[(1 - y) * (z // 4)]

        def cot_ready(i):
            @pl.when(i > 0)
            def _():
                drain_recv(cot_all.at[rows(i * 128, 128)], ct_r.at[i])

        def back(i):
            return lax.dot_general(
                cot_all[rows(i * 128, 128), :], wout[...], (((1,), (1,)), ((), ())),
                preferred_element_type=F32,
            )

        def dpre_of(i, total):
            return (total * slope[i]).astype(BF16)

        def over_tokens(left, right):
            return lax.dot_general(
                left, right, (((0,), (0,)), ((), ())), preferred_element_type=F32
            )

        def grads(i):
            @pl.when(i == 4)
            def _():
                for h in range(2):
                    gout_ref[h * 384 : h * 384 + 384, :] = over_tokens(hid[h], cot_all[...])

        pipeline(
            cot_ready, back, dpre_of, grads, dpre,
            keep2, give2, sib_in2, summed2, rs_in2,
            sb2_s, sb2_r, rs2_s, rs2_r, ag2_s, ag2_r, rl2_s, rl2_r,
        )
        for h in range(2):
            gin_ref[:, h * 384 : h * 384 + 384] = over_tokens(tok_all[...], dpre[h])
        drain_send(cot_all.at[rows(0, 896)], ct_s)

    @pl.when(y >= 2)
    def _():
        gin_ref[...] = jnp.zeros_like(gin_ref)
        gout_ref[...] = jnp.zeros_like(gout_ref)

    for which in range(3):
        @pl.when(y != which // 2)
        def _(which=which):
            cot_y_copy(which).wait_send()

    @pl.loop(1, 4)
    def _(j):
        k = (y + j) % 4
        y_copy(0, k, 0).wait_send()

        @pl.when(y == 0)
        def _():
            y_copy(1, k, 0).wait_send()

    drain_send(z_in.at[pl.ds(0, 7)], zin_s)
    drain_send(tok_all.at[rows(0, 992)], tok_s)


def shards(tokens, in_weight, out_weight):
    vmem = pl.BlockSpec(memory_space=pltpu.VMEM)
    hbm = pl.BlockSpec(memory_space=pl.ANY)
    dma = pltpu.SemaphoreType.DMA
    one = dma(())
    block = pltpu.VMEM((8, 128, 384), BF16)
    flat = pltpu.VMEM((1024, 384), BF16)
    return pl.pallas_call(
        kernel,
        out_shape=(
            jax.ShapeDtypeStruct((32, 384), BF16),
            jax.ShapeDtypeStruct((384, 768), F32),
            jax.ShapeDtypeStruct((768, 384), F32),
        ),
        in_specs=[hbm, hbm, hbm],
        out_specs=(vmem, vmem, vmem),
        scratch_shapes=[
            pltpu.VMEM((384, 768), BF16),
            pltpu.VMEM((768, 384), BF16),
            flat,
            pltpu.VMEM((8, 16, 384), F32),
            pltpu.VMEM((2, 1024, 384), BF16),
            block,
            block,
            pltpu.VMEM((2, 4, 32, 384), BF16),
            pltpu.VMEM((5, 32, 384), BF16),
            pltpu.VMEM((3, 32, 384), BF16),
            pltpu.VMEM((2, 128, 384), BF16),
            flat,
            pltpu.VMEM((2, 1024, 384), BF16),
        ]
        + [block, block, block, flat, flat] * 2
        + [
            dma((3,)),
            one, dma((8,)),
            one, one,
            dma((2, 4)), dma((5,)),
            dma((3,)), dma((2, 4)),
            one, dma((8,)),
        ]
        + [one, dma((8,))] * 8,
        compiler_params=pltpu.CompilerParams(
            collective_id=0, has_side_effects=True, vmem_limit_bytes=60 * 1024 * 1024
        ),
        cost_estimate=pl.CostEstimate(
            flops=5 * 2 * 1024 * 384 * 768, bytes_accessed=4_000_000, transcendentals=100_000
        ),
    )(tokens, in_weight, out_weight)


def solution(mesh):
    in_specs = (P("tensor", "dp"), P("dp", "tensor"), P("tensor", "dp"))
    out_specs = (P("tensor", "dp"), P("dp", "tensor"), P("tensor", "dp"))
    return jax.shard_map(shards, mesh=mesh, in_specs=in_specs, out_specs=out_specs, check_vma=False)
```

time: 404 us -> 116 us (0.29)
  waiting for transfers between devices: 237 us -> 0 us
  Pallas kernels: 0 us -> 111 us
  blocking collectives: 109 us -> 0 us
  between operations: 14 us -> 0.64 us
  starting transfers between devices: 12.1 us -> 0 us
  matrix products: 12 us -> 0 us
  other arithmetic: 9.77 us -> 0 us
  local copies, waits for them, and re-layouts: 9.71 us -> 4.82 us
    reduce_scatter x2 -> x0, waiting for transfers between devices: 136 us -> none  [the longest x1 72.2 us: shards(): lax.psum_scatter(jnp.dot(row_block, in_weight, preferred_element_type=jnp...]
    pallas_call x0 -> x1, Pallas kernels: none -> 111 us  [shards(): pl.pallas_call(kernel, out_shape=(jax.ShapeDtypeStruct((32, 384), BF16),...]
    all_gather x1 -> x0, blocking collectives: 80.4 us -> none  [shards(): everything = lax.all_gather(tokens, 'tensor', axis=0, tiled=True)]
    all_gather x2 -> x0, waiting for transfers between devices: 78.9 us -> none  [the longest x1 42.1 us: shards(): preact_all = lax.all_gather(preact_local, 'dp', axis=0, tiled=True)]
    all_to_all x1 -> x0, blocking collectives: 28.7 us -> none  [shards(): lax.all_to_all(outbound, 'tensor', split_axis=0, concat_axis=1, tiled=True)]
    all_to_all x1 -> x0, waiting for transfers between devices: 22.8 us -> none  [shards(): lax.all_to_all(partial_value[None].astype(jnp.bfloat16), 'tensor', split_...]
    dot_general x5 -> x0, matrix products: 12 us -> none  [the longest x1 3.22 us: shards(): lax.dot_general(hidden, returned, (((0,), (0,)), ((), ())), preferred_ele...]
    all_to_all x1 -> x0, starting transfers between devices: 12 us -> none  [shards(): lax.all_to_all(partial_value[None].astype(jnp.bfloat16), 'tensor', split_...]
  transfers between devices with their start and end apart: 5 -> 0, of which waited for: 5 -> 0; matrix products, arithmetic and copies ran while one was open for 1% -> 0% of each run, Pallas kernels for 0% -> 0%
where the time goes in v2:
time: 116 us
  Pallas kernels  111 us (96%)
  local copies, waits for them, and re-layouts  4.82 us (4%)
    pallas_call x1, Pallas kernels, shards(): pl.pallas_call(kernel, out_shape=(jax.ShapeDtypeStruct((32, 384), BF16),...  111 us
    unnamed x5, local copies, waits for them, and re-layouts  4.82 us

profile of v2, /device:TPU:1, one launch (start us, length us, event | category | flops | bytes accessed | tf_op | source)
XLA Modules:
  0.0 116.2 jit_solution(4105545069096033093)
XLA Ops:
  0.6 110.7 %shard_map.58 = (bf16[32,384]{1,0:T(8,128)(2,1)}, f32[384,768]{1,0:T(8,128)}, f32[768,384]{1,0:T(8,128)}) custom-call(bf16[32,384]{1,0:T(8,128)(2,1)} %tok_hbm.1, bf16[384,768]{1,0:T(8,128)(2,1)} %win_hbm.1, bf16[768,384]{1,0:T(8,128)(2,1)} %wout_hbm.1), custom_call_target="tpu_custom_call" | custom-call | flops 3019898880 | bytes 4000000 | tf_op jit(solution)/shard_map/pallas_call | solution.py:405
  111.3 1.3 %copy.9 = bf16[32,384]{1,0:T(8,128)(2,1)} copy(bf16[32,384]{1,0:T(8,128)(2,1)} %get-tuple-element.6) | data formatting | bytes 49152
  112.7 0.0 copy-start
  112.7 2.5 %copy.10 = f32[384,768]{1,0:T(8,128)} copy(f32[384,768]{1,0:T(8,128)} %get-tuple-element.7) | data formatting | bytes 2359296
  115.1 0.0 copy-done
  115.2 1.0 copy.11
Async XLA Ops:
  112.7 2.5 %copy-start = (f32[768,384]{1,0:T(8,128)S(1)}, f32[768,384]{1,0:T(8,128)}, u32[]{:S(2)}) copy-start(f32[768,384]{1,0:T(8,128)} %get-tuple-element.8) | copy-start | bytes 3538948

commit v3 on v2

--- a/solution.py
+++ b/solution.py
@@ -10,7 +10,9 @@
 MESH = pl.DeviceIdType.MESH
 BF16 = jnp.bfloat16
 F32 = jnp.float32
-LAG_SUM, LAG_HID, LAG_ALL, LAG_USE = 1, 4, 7, 8
+FORWARD_LAGS = (1, 4, 7, 9)
+BACKWARD_LAGS = (1, 6, 11, 13)
+FAR = 3
 
 
 def smooth_gate(values):
@@ -24,18 +26,25 @@
     )
 
 
+def over_tokens(left, right):
+    return lax.dot_general(
+        left, right, (((0,), (0,)), ((), ())), preferred_element_type=F32
+    )
+
+
 def rows(start, size, step=None):
     return pl.ds(pl.multiple_of(start, step or size), size)
 
 
 def kernel(
     tok_hbm, win_hbm, wout_hbm,
-    teacher_ref, gin_ref, gout_ref,
-    win, wout, tok_all, slope, hid, contrib, z_in, y_out, y_in,
-    cots, cot_y, cot_all, dpre,
+    teacher_ref, tok_all, dpre, gout_ref,
+    win, wout, slope, hid, contrib, z_in, y_out, y_in,
+    cots, cot_y, cot_far, cot_all,
     keep, give, sib_in, summed, rs_in,
     keep2, give2, sib_in2, summed2, rs_in2,
-    wsem, tok_s, tok_r, zin_s, zin_r, yin_s, yin_r, cy_s, cy_r, ct_s, ct_r,
+    wsem, tok_s, tok_r, far_r, zin_s, zin_r, yin_s, yin_r, cy_s, cy_r, ct_s, ct_r,
+    cfar_s, cfar_r, cfw_s, cfw_r,
     sb_s, sb_r, rs_s, rs_r, ag_s, ag_r, rl_s, rl_r,
     sb2_s, sb2_r, rs2_s, rs2_r, ag2_s, ag2_r, rl2_s, rl2_r,
 ):
@@ -95,35 +104,42 @@
     w0.wait()
     pl.semaphore_wait(barrier, 18)
 
-    def chunk_to(i, k, src, all_ref, s_sem, r_sem):
-        return remote(
-            src, all_ref.at[rows(i * 128 + k * 32, 32)], s_sem, r_sem.at[i],
+    @pl.loop(1, FAR + 1)
+    def _(i):
+        remote(
+            mine, tok_all.at[rows(i * 128 + y * 32, 32)], tok_s, tok_r.at[i],
             {"tensor": y * 8 + along_z(i)},
-        )
-
-    @pl.loop(1, 4)
+        ).start()
+
+    @pl.loop(0, 3)
     def _(j):
-        k = (y + 1 + j % 3) % 4
+        k = (y + 1 + (j + 1) % 3) % 4
         remote(mine, mine, tok_s, tok_r.at[0], {"tensor": k * 8 + z}).start()
 
-    @pl.loop(1, 8)
-    def _(i):
-        chunk_to(i, y, mine, tok_all, tok_s, tok_r).start()
-
     drain_recv(tok_all.at[rows(0, 96)], tok_r.at[0])
 
-    @pl.loop(1, 8)
-    def _(i):
-        @pl.loop(1, 4)
+    @pl.loop(FAR + 1, 8)
+    def _(i):
+        remote(
+            tok_all.at[rows(0, 128)], tok_all.at[rows(i * 128, 128)], tok_s, tok_r.at[i],
+            {"tensor": y * 8 + along_z(i)},
+        ).start()
+
+    @pl.loop(1, FAR + 1)
+    def _(i):
+        part = tok_all.at[rows(i * 128 + y * 32, 32)]
+        drain_recv(part, tok_r.at[i])
+
+        @pl.loop(0, 3)
         def _(j):
-            k = (y + j) % 4
-            chunk_to(i, k, tok_all.at[rows(k * 32, 32)], tok_all, tok_s, tok_r).start()
+            k = (y + 1 + (j + 1) % 3) % 4
+            remote(part, part, tok_s, far_r.at[i], {"tensor": k * 8 + z}).start()
 
     w1.wait()
     w2.wait()
 
     def pipeline(
-        ready, block, finish, use, full_buf,
+        lags, ready, block, finish, use, full_buf,
         keep, give, sib_in, summed, rs_in, sb_s, sb_r, rs_s, rs_r, ag_s, ag_r, rl_s, rl_r,
     ):
         def sib_copy(i):
@@ -133,20 +149,41 @@
             place = full_buf.at[core, rows(i * 128, 128)]
             return remote(place, place, rl_s, rl_r.at[i], {"dp": sib})
 
-        @pl.loop(0, 8 + LAG_USE)
+        lag_sum, lag_hid, lag_all, lag_use = lags
+
+        @pl.loop(0, 8 + lag_use)
         def _(s):
-            @pl.when(s < 8)
-            def _():
-                ready(s)
-                term = block(s).astype(BF16)
-                first, second = term[:, :384], term[:, 384:]
-                keep[s] = jnp.where(core == 0, first, second)
-                give[s] = jnp.where(core == 0, second, first)
-                sib_copy(s).start()
-
-            @pl.when((s >= LAG_SUM) & (s < LAG_SUM + 8))
-            def _():
-                i = s - LAG_SUM
+            @pl.when(s >= lag_use)
+            def _():
+                i = s - lag_use
+                relay(i).wait_recv()
+                use(i)
+
+            @pl.when((s >= lag_all) & (s < lag_all + 8))
+            def _():
+                i = s - lag_all
+                drain_recv(full_buf.at[core, rows(i * 128, 112, 128)], ag_r.at[i])
+                relay(i).start()
+
+            @pl.when((s >= lag_hid) & (s < lag_hid + 8))
+            def _():
+                i = s - lag_hid
+                drain_recv(rs_in.at[rows(i * 128, 112, 128)], rs_r.at[i])
+                total = jnp.zeros((16, 384), F32)
+                for c in range(8):
+                    total = total + rs_in[rows(i * 128 + c * 16, 16), :].astype(F32)
+                own = rows(i * 128 + chip * 16, 16)
+                full_buf[core, own, :] = finish(i, total)
+                place = full_buf.at[core, own]
+
+                @pl.loop(1, 8)
+                def _(j):
+                    c = (chip + j) % 8
+                    remote(place, place, ag_s, ag_r.at[i], {"dp": c * 2 + core}).start()
+
+            @pl.when((s >= lag_sum) & (s < lag_sum + 8))
+            def _():
+                i = s - lag_sum
                 sib_copy(i).wait_recv()
                 total = (keep[i].astype(F32) + sib_in[i].astype(F32)).astype(BF16)
                 summed[rows(i * 128, 128), :] = total
@@ -163,43 +200,31 @@
                 own = rows(i * 128 + chip * 16, 16)
                 rs_in[own, :] = summed[own, :]
 
-            @pl.when((s >= LAG_HID) & (s < LAG_HID + 8))
-            def _():
-                i = s - LAG_HID
-                drain_recv(rs_in.at[rows(i * 128, 112, 128)], rs_r.at[i])
-                total = jnp.zeros((16, 384), F32)
-                for c in range(8):
-                    total = total + rs_in[rows(i * 128 + c * 16, 16), :].astype(F32)
-                own = rows(i * 128 + chip * 16, 16)
-                full_buf[core, own, :] = finish(i, total)
-                place = full_buf.at[core, own]
-
-                @pl.loop(1, 8)
-                def _(j):
-                    c = (chip + j) % 8
-                    remote(place, place, ag_s, ag_r.at[i], {"dp": c * 2 + core}).start()
-
-            @pl.when((s >= LAG_ALL) & (s < LAG_ALL + 8))
-            def _():
-                i = s - LAG_ALL
-                drain_recv(full_buf.at[core, rows(i * 128, 112, 128)], ag_r.at[i])
-                relay(i).start()
-
-            @pl.when(s >= LAG_USE)
-            def _():
-                i = s - LAG_USE
-                relay(i).wait_recv()
-                use(i)
+            @pl.when(s < 8)
+            def _():
+                ready(s)
+                term = block(s).astype(BF16)
+                first, second = term[:, :384], term[:, 384:]
+                keep[s] = jnp.where(core == 0, first, second)
+                give[s] = jnp.where(core == 0, second, first)
+                sib_copy(s).start()
 
         drain_send(give, sb_s)
         drain_send(summed.at[rows(0, 896)], rs_s)
         drain_send(full_buf.at[0, rows(0, 896)], ag_s)
         drain_send(full_buf.at[0], rl_s)
 
+    def ready_of(all_ref, near_r, far_r, i):
+        @pl.when(i > FAR)
+        def _():
+            drain_recv(all_ref.at[rows(i * 128, 128)], near_r.at[i])
+
+        @pl.when((i > 0) & (i <= FAR))
+        def _():
+            drain_recv(all_ref.at[rows(i * 128, 96, 128)], far_r.at[i])
+
     def tok_ready(i):
-        @pl.when(i > 0)
-        def _():
-            drain_recv(tok_all.at[rows(i * 128, 128)], tok_r.at[i])
+        ready_of(tok_all, tok_r, far_r, i)
 
     def up(i):
         return jnp.dot(tok_all[rows(i * 128, 128), :], win[...], preferred_element_type=F32)
@@ -225,7 +250,7 @@
             remote(contrib.at[i], z_in.at[z], zin_s, zin_r, {"tensor": y * 8 + dst}).start()
 
     pipeline(
-        tok_ready, up, hidden_of, down, hid,
+        FORWARD_LAGS, tok_ready, up, hidden_of, down, hid,
         keep, give, sib_in, summed, rs_in, sb_s, sb_r, rs_s, rs_r, ag_s, ag_r, rl_s, rl_r,
     )
 
@@ -308,18 +333,20 @@
         def _(which=which):
             cot_y[which % 2, rows(y * 32, 32), :] = cots[which]
 
+    @pl.loop(1, FAR + 1)
+    def _(i):
+        z_to = along_z(i)
+        for row in range(2):
+            kind = z_to // 4 if row == 0 else 2
+            remote(
+                cots.at[kind], cot_far.at[i, rows(row * 32, 32)], cfar_s, cfar_r.at[i],
+                {"tensor": y * 8 + z_to},
+            ).start()
+
     teacher_ref[...] = full.astype(BF16)
 
     @pl.when(y < 2)
     def _():
-        def cot_chunk(i, k):
-            kind = (1 - y) * (along_z(i) // 4)
-            return chunk_to(i, k, cot_y.at[kind, rows(k * 32, 32)], cot_all, ct_s, ct_r)
-
-        @pl.loop(1, 8)
-        def _(i):
-            cot_chunk(i, y).start()
-
         @pl.loop(1, 4)
         def _(j):
             k = (y + j) % 4
@@ -330,18 +357,37 @@
             def _():
                 drain_recv(part, cy_r.at[1, k])
 
-        @pl.loop(1, 8)
+        @pl.loop(FAR + 1, 8)
         def _(i):
-            @pl.loop(1, 4)
-            def _(j):
-                cot_chunk(i, (y + j) % 4).start()
+            kind = (1 - y) * (along_z(i) // 4)
+            remote(
+                cot_y.at[kind], cot_all.at[rows(i * 128, 128)], ct_s, ct_r.at[i],
+                {"tensor": y * 8 + along_z(i)},
+            ).start()
 
         cot_all[rows(0, 128), :] = cot_y[(1 - y) * (z // 4)]
 
+    @pl.loop(1, FAR + 1)
+    def _(i):
+        drain_recv(cot_far.at[i], cfar_r.at[i])
+        place = rows(i * 128 + y * 32, 32)
+        for row in range(2):
+            part = cot_far.at[i, rows(row * 32, 32)]
+
+            @pl.when(y != row)
+            def _(part=part, row=row):
+                remote(
+                    part, cot_all.at[place], cfw_s, cfw_r.at[i], {"tensor": row * 8 + z}
+                ).start()
+
+            @pl.when(y == row)
+            def _(part=part):
+                cot_all[place, :] = part[...]
+
+    @pl.when(y < 2)
+    def _():
         def cot_ready(i):
-            @pl.when(i > 0)
-            def _():
-                drain_recv(cot_all.at[rows(i * 128, 128)], ct_r.at[i])
+            ready_of(cot_all, ct_r, cfw_r, i)
 
         def back(i):
             return lax.dot_general(
@@ -352,11 +398,6 @@
         def dpre_of(i, total):
             return (total * slope[i]).astype(BF16)
 
-        def over_tokens(left, right):
-            return lax.dot_general(
-                left, right, (((0,), (0,)), ((), ())), preferred_element_type=F32
-            )
-
         def grads(i):
             @pl.when(i == 4)
             def _():
@@ -364,18 +405,17 @@
                     gout_ref[h * 384 : h * 384 + 384, :] = over_tokens(hid[h], cot_all[...])
 
         pipeline(
-            cot_ready, back, dpre_of, grads, dpre,
+            BACKWARD_LAGS, cot_ready, back, dpre_of, grads, dpre,
             keep2, give2, sib_in2, summed2, rs_in2,
             sb2_s, sb2_r, rs2_s, rs2_r, ag2_s, ag2_r, rl2_s, rl2_r,
         )
-        for h in range(2):
-            gin_ref[:, h * 384 : h * 384 + 384] = over_tokens(tok_all[...], dpre[h])
-        drain_send(cot_all.at[rows(0, 896)], ct_s)
+        drain_send(cot_all.at[rows(0, 128 * (7 - FAR))], ct_s)
+        drain_send(cot_all.at[rows(0, 32 * FAR)], cfw_s)
 
     @pl.when(y >= 2)
     def _():
-        gin_ref[...] = jnp.zeros_like(gin_ref)
         gout_ref[...] = jnp.zeros_like(gout_ref)
+        drain_send(cot_all.at[rows(0, 64 * FAR)], cfw_s)
 
     for which in range(3):
         @pl.when(y != which // 2)
@@ -391,30 +431,58 @@
         def _():
             y_copy(1, k, 0).wait_send()
 
+    drain_send(cot_all.at[rows(0, 64 * FAR)], cfar_s)
     drain_send(z_in.at[pl.ds(0, 7)], zin_s)
     drain_send(tok_all.at[rows(0, 992)], tok_s)
 
 
+def finish_kernel(
+    teacher_ref, tok_ref, dpre_ref, gout_ref, teacher_out, gin_out, gout_out, gin, sem
+):
+    t = lax.axis_index("tensor")
+    w0 = pltpu.make_async_copy(gout_ref, gout_out, sem.at[0])
+    w0.start()
+    wt = pltpu.make_async_copy(teacher_ref, teacher_out, sem.at[3])
+    wt.start()
+    copies = [w0, wt]
+    for h in range(2):
+        part = pl.ds(h * 384, 384)
+
+        @pl.when(t < 16)
+        def _(h=h):
+            gin[:, h * 384 : h * 384 + 384] = over_tokens(tok_ref[...], dpre_ref[h])
+
+        @pl.when(t >= 16)
+        def _(h=h):
+            gin[:, h * 384 : h * 384 + 384] = jnp.zeros((384, 384), F32)
+
+        w1 = pltpu.make_async_copy(gin.at[:, part], gin_out.at[:, part], sem.at[1 + h])
+        w1.start()
+        copies.append(w1)
+    for w1 in copies:
+        w1.wait()
+
+
 def shards(tokens, in_weight, out_weight):
     vmem = pl.BlockSpec(memory_space=pltpu.VMEM)
-    hbm = pl.BlockSpec(memory_space=pl.ANY)
+    hbm = pl.BlockSpec(memory_space=pltpu.HBM)
     dma = pltpu.SemaphoreType.DMA
     one = dma(())
     block = pltpu.VMEM((8, 128, 384), BF16)
     flat = pltpu.VMEM((1024, 384), BF16)
-    return pl.pallas_call(
+    teacher, tok_all, dpre, grad_out = pl.pallas_call(
         kernel,
         out_shape=(
             jax.ShapeDtypeStruct((32, 384), BF16),
-            jax.ShapeDtypeStruct((384, 768), F32),
+            jax.ShapeDtypeStruct((1024, 384), BF16),
+            jax.ShapeDtypeStruct((2, 1024, 384), BF16),
             jax.ShapeDtypeStruct((768, 384), F32),
         ),
         in_specs=[hbm, hbm, hbm],
-        out_specs=(vmem, vmem, vmem),
+        out_specs=(vmem, vmem, vmem, vmem),
         scratch_shapes=[
             pltpu.VMEM((384, 768), BF16),
             pltpu.VMEM((768, 384), BF16),
-            flat,
             pltpu.VMEM((8, 16, 384), F32),
             pltpu.VMEM((2, 1024, 384), BF16),
             block,
@@ -423,26 +491,42 @@
             pltpu.VMEM((5, 32, 384), BF16),
             pltpu.VMEM((3, 32, 384), BF16),
             pltpu.VMEM((2, 128, 384), BF16),
+            pltpu.VMEM((8, 64, 384), BF16),
             flat,
-            pltpu.VMEM((2, 1024, 384), BF16),
         ]
         + [block, block, block, flat, flat] * 2
         + [
             dma((3,)),
-            one, dma((8,)),
+            one, dma((8,)), dma((8,)),
             one, one,
             dma((2, 4)), dma((5,)),
             dma((3,)), dma((2, 4)),
             one, dma((8,)),
+            one, dma((8,)), one, dma((8,)),
         ]
         + [one, dma((8,))] * 8,
         compiler_params=pltpu.CompilerParams(
-            collective_id=0, has_side_effects=True, vmem_limit_bytes=60 * 1024 * 1024
+            collective_id=0, has_side_effects=True, vmem_limit_bytes=32 * 1024 * 1024
         ),
         cost_estimate=pl.CostEstimate(
-            flops=5 * 2 * 1024 * 384 * 768, bytes_accessed=4_000_000, transcendentals=100_000
+            flops=4 * 2 * 1024 * 384 * 768, bytes_accessed=4_000_000, transcendentals=100_000
         ),
-    )(tokens, in_weight, out_weight)
+    )(*[pltpu.with_memory_space_constraint(v, pltpu.HBM) for v in (tokens, in_weight, out_weight)])
+    return pl.pallas_call(
+        finish_kernel,
+        out_shape=(
+            jax.ShapeDtypeStruct((32, 384), BF16),
+            jax.ShapeDtypeStruct((384, 768), F32),
+            jax.ShapeDtypeStruct((768, 384), F32),
+        ),
+        in_specs=[vmem, vmem, vmem, vmem],
+        out_specs=(hbm, hbm, hbm),
+        scratch_shapes=[pltpu.VMEM((384, 768), F32), dma((4,))],
+        compiler_params=pltpu.CompilerParams(vmem_limit_bytes=16 * 1024 * 1024),
+        cost_estimate=pl.CostEstimate(
+            flops=2 * 1024 * 384 * 768, bytes_accessed=4_000_000, transcendentals=0
+        ),
+    )(teacher, tok_all, dpre, grad_out)
 
 
 def solution(mesh):

time: 116 us -> 106 us (0.914)
  Pallas kernels: 111 us -> 105 us
  local copies, waits for them, and re-layouts: 4.82 us -> 0 us
    pallas_call x1, Pallas kernels: 111 us -> 103 us  [shards(): pl.pallas_call(kernel, out_shape=(jax.ShapeDtypeStruct((32, 384), BF16),...]
    unnamed x5 -> x0, local copies, waits for them, and re-layouts: 4.82 us -> none
    pallas_call x0 -> x1, Pallas kernels: none -> 2.06 us  [shards(): pl.pallas_call(finish_kernel, out_shape=(jax.ShapeDtypeStruct((32, 384),...]
where the time goes in v3:
time: 106 us; the launch traced here: 105 us
  Pallas kernels  105 us (99%)
    pallas_call x1, Pallas kernels, shards(): pl.pallas_call(kernel, out_shape=(jax.ShapeDtypeStruct((32, 384), BF16),...  103 us

profile of v3, /device:TPU:1, one launch (start us, length us, event | category | flops | bytes accessed | tf_op | source)
XLA Modules:
  0.0 105.5 jit_solution(14462512623607322760)
XLA Ops:
  0.6 102.8 %shard_map.58 = (bf16[32,384]{1,0:T(8,128)(2,1)S(1)}, bf16[1024,384]{1,0:T(8,128)(2,1)S(1)}, bf16[2,1024,384]{2,1,0:T(8,128)(2,1)S(1)}, f32[768,384]{1,0:T(8,128)S(1)}) custom-call(bf16[32,384]{1,0:T(8,128)(2,1)} %tok_hbm.1, bf16[384,768]{1,0:T(8,128)(2,1)} %win_hbm.1, bf16[768,384]{1,0:T(8,128)(2,1)} %wout_hbm.1), custom_call_target="tpu_custom_call" | custom-call | flops 2415919104 | bytes 4000000 | tf_op jit(solution)/shard_map/pallas_call | solution.py:473
  103.4 2.1 %shard_map.59 = (bf16[32,384]{1,0:T(8,128)(2,1)}, f32[384,768]{1,0:T(8,128)}, f32[768,384]{1,0:T(8,128)}) custom-call(bf16[32,384]{1,0:T(8,128)(2,1)S(1)} %get-tuple-element.7.teacher_ref, bf16[1024,384]{1,0:T(8,128)(2,1)S(1)} %get-tuple-element.8.tok_ref, bf16[2,1024,384]{2,1,0:T(8,128)(2,1)S(1)} %get-tuple-element.9.dpre_ref, ...), custom_call_target="tpu_custom_call" | custom-call | flops 603979776 | bytes 4000000 | tf_op jit(solution)/shard_map/pallas_call | solution.py:515

commit v4 on v3

--- a/solution.py
+++ b/solution.py
@@ -10,8 +10,8 @@
 MESH = pl.DeviceIdType.MESH
 BF16 = jnp.bfloat16
 F32 = jnp.float32
-FORWARD_LAGS = (1, 4, 7, 9)
-BACKWARD_LAGS = (1, 6, 11, 13)
+FORWARD_LAGS = (1, 4, 7, 8)
+BACKWARD_LAGS = (1, 6, 11, 12)
 FAR = 3
 
 
@@ -399,7 +399,7 @@
             return (total * slope[i]).astype(BF16)
 
         def grads(i):
-            @pl.when(i == 4)
+            @pl.when(i == 0)
             def _():
                 for h in range(2):
                     gout_ref[h * 384 : h * 384 + 384, :] = over_tokens(hid[h], cot_all[...])

time: 106 us -> 104 us (0.981)
  Pallas kernels: 105 us -> 103 us
    pallas_call x1, Pallas kernels: 103 us -> 101 us  [shards(): pl.pallas_call(kernel, out_shape=(jax.ShapeDtypeStruct((32, 384), BF16),...]
where the time goes in v4:
time: 104 us
  Pallas kernels  103 us (99%)
    pallas_call x1, Pallas kernels, shards(): pl.pallas_call(kernel, out_shape=(jax.ShapeDtypeStruct((32, 384), BF16),...  101 us

profile of v4, /device:TPU:1, one launch (start us, length us, event | category | flops | bytes accessed | tf_op | source)
XLA Modules:
  0.0 103.9 jit_solution(1868883891721939998)
XLA Ops:
  0.6 101.2 %shard_map.58 = (bf16[32,384]{1,0:T(8,128)(2,1)S(1)}, bf16[1024,384]{1,0:T(8,128)(2,1)S(1)}, bf16[2,1024,384]{2,1,0:T(8,128)(2,1)S(1)}, f32[768,384]{1,0:T(8,128)S(1)}) custom-call(bf16[32,384]{1,0:T(8,128)(2,1)} %tok_hbm.1, bf16[384,768]{1,0:T(8,128)(2,1)} %win_hbm.1, bf16[768,384]{1,0:T(8,128)(2,1)} %wout_hbm.1), custom_call_target="tpu_custom_call" | custom-call | flops 2415919104 | bytes 4000000 | tf_op jit(solution)/shard_map/pallas_call | solution.py:473
  101.9 2.1 %shard_map.59 = (bf16[32,384]{1,0:T(8,128)(2,1)}, f32[384,768]{1,0:T(8,128)}, f32[768,384]{1,0:T(8,128)}) custom-call(bf16[32,384]{1,0:T(8,128)(2,1)S(1)} %get-tuple-element.7.teacher_ref, bf16[1024,384]{1,0:T(8,128)(2,1)S(1)} %get-tuple-element.8.tok_ref, bf16[2,1024,384]{2,1,0:T(8,128)(2,1)S(1)} %get-tuple-element.9.dpre_ref, ...), custom_call_target="tpu_custom_call" | custom-call | flops 603979776 | bytes 4000000 | tf_op jit(solution)/shard_map/pallas_call | solution.py:515

commit v5 on v4

--- a/solution.py
+++ b/solution.py
@@ -104,17 +104,17 @@
     w0.wait()
     pl.semaphore_wait(barrier, 18)
 
+    @pl.loop(0, 3)
+    def _(j):
+        k = (y + 1 + (j + 1) % 3) % 4
+        remote(mine, mine, tok_s, tok_r.at[0], {"tensor": k * 8 + z}).start()
+
     @pl.loop(1, FAR + 1)
     def _(i):
         remote(
             mine, tok_all.at[rows(i * 128 + y * 32, 32)], tok_s, tok_r.at[i],
             {"tensor": y * 8 + along_z(i)},
         ).start()
-
-    @pl.loop(0, 3)
-    def _(j):
-        k = (y + 1 + (j + 1) % 3) % 4
-        remote(mine, mine, tok_s, tok_r.at[0], {"tensor": k * 8 + z}).start()
 
     drain_recv(tok_all.at[rows(0, 96)], tok_r.at[0])
 

time: 104 us -> 104 us (level)
  no operation moved by 1% of the time
where the time goes in v5:
time: 104 us
  Pallas kernels  104 us (100%)
    pallas_call x1, Pallas kernels, shards(): pl.pallas_call(kernel, out_shape=(jax.ShapeDtypeStruct((32, 384), BF16),...  102 us

profile of v5, /device:TPU:1, one launch (start us, length us, event | category | flops | bytes accessed | tf_op | source)
XLA Modules:
  0.0 104.3 jit_solution(5112762238269853122)
XLA Ops:
  0.6 101.7 %shard_map.58 = (bf16[32,384]{1,0:T(8,128)(2,1)S(1)}, bf16[1024,384]{1,0:T(8,128)(2,1)S(1)}, bf16[2,1024,384]{2,1,0:T(8,128)(2,1)S(1)}, f32[768,384]{1,0:T(8,128)S(1)}) custom-call(bf16[32,384]{1,0:T(8,128)(2,1)} %tok_hbm.1, bf16[384,768]{1,0:T(8,128)(2,1)} %win_hbm.1, bf16[768,384]{1,0:T(8,128)(2,1)} %wout_hbm.1), custom_call_target="tpu_custom_call" | custom-call | flops 2415919104 | bytes 4000000 | tf_op jit(solution)/shard_map/pallas_call | solution.py:473
  102.3 2.1 %shard_map.59 = (bf16[32,384]{1,0:T(8,128)(2,1)}, f32[384,768]{1,0:T(8,128)}, f32[768,384]{1,0:T(8,128)}) custom-call(bf16[32,384]{1,0:T(8,128)(2,1)S(1)} %get-tuple-element.7.teacher_ref, bf16[1024,384]{1,0:T(8,128)(2,1)S(1)} %get-tuple-element.8.tok_ref, bf16[2,1024,384]{2,1,0:T(8,128)(2,1)S(1)} %get-tuple-element.9.dpre_ref, ...), custom_call_target="tpu_custom_call" | custom-call | flops 603979776 | bytes 4000000 | tf_op jit(solution)/shard_map/pallas_call | solution.py:515
